TPU v7x, 512 devices: a whole 4x4x16 slice. The times are simulated.
512 devices in a mesh: ka: 64 (over z, y), row: 8 (over x, core).
Axes of the slice: x: 4, y: 4, z: 16, core: 2. Of those that a mesh axis runs over, the one named last changes fastest.
Arguments:
- inputs: bfloat16 [256, 16384], P(None, 'ka'), may hold values from -16 to 16
- weight: bfloat16 [18432, 16384], P('row', 'ka'), as said below
- out_grad: bfloat16 [256, 18432], P('ka', 'row'), may hold values from -16 to 16
Outputs:
- projected: bfloat16 [256, 18432], P('ka', 'row')
- input_grad: bfloat16 [256, 16384], P('row', 'ka')
- weight_grad: bfloat16 [18432, 16384], P('row', 'ka')
Inputs may be any that keep to these rules, and one draw needn't show every extreme that they name: Every entry is finite and no row of the weight is all zero.
All inputs are finite; a program needn't handle non-finite values.
Results may differ from a plain program's by a relative error of at most 0.0049.
Values may be sent and summed in bfloat16 or wider, within the bound.
A program may use at most 64 MiB of HBM per device.

v0:
```python
import math

import jax
import jax.numpy as jnp
from jax import lax
from jax.sharding import PartitionSpec as P

LEVELS = 7


def smooth_grid(wide, peak):
    step = (peak / LEVELS)[:, None]
    smooth = wide - step / (2.0 * math.pi) * jnp.sin(2.0 * math.pi * wide / step)
    return smooth.astype(jnp.bfloat16)


def local(inputs, weight, out_grad):
    wide = weight.astype(jnp.float32)
    peak = lax.pmax(jnp.max(jnp.abs(wide), axis=1), "ka")
    quantized = smooth_grid(wide, peak)
    projected = lax.psum_scatter(
        lax.dot_general(
            inputs, quantized, (((1,), (1,)), ((), ())), preferred_element_type=jnp.float32
        ),
        "ka",
        scatter_dimension=0,
        tiled=True,
    ).astype(jnp.bfloat16)
    full_grad = lax.all_gather(out_grad, "ka", axis=0, tiled=True)
    input_part = jnp.dot(full_grad, quantized, preferred_element_type=jnp.float32)
    weight_part = lax.dot_general(
        full_grad, inputs, (((0,), (0,)), ((), ())), preferred_element_type=jnp.float32
    )
    input_grad = lax.psum_scatter(input_part, "row", scatter_dimension=0, tiled=True).astype(
        jnp.bfloat16
    )
    weight_grad = (weight_part * (1.0 / math.sqrt(inputs.shape[0]))).astype(jnp.bfloat16)
    return (projected, input_grad, weight_grad)


def solution(mesh):
    placed = (P(None, "ka"), P("row", "ka"), P("ka", "row"))
    return jax.shard_map(
        local,
        mesh=mesh,
        in_specs=placed,
        out_specs=(P("ka", "row"), P("row", "ka"), P("row", "ka")),
        check_vma=False,
    )
```

profile of v0, /device:TPU:1, one launch (start us, length us, event | category | flops | bytes accessed | tf_op | source)
XLA Modules:
  0.0 663.7 jit_solution(18051215905736596929)
XLA Ops:
  7.2 0.0 copy-start
  7.2 0.0 all-gather.3.cloned.1.call-start
  7.2 0.7 all-gather.3.cloned.1.call-update
  7.9 0.0 reduce-scatter.5.cloned.1.call-start
  8.0 1.7 fusion.1
  9.6 231.7 %pmax.7 = f32[2304]{0:T(1024)S(1)} all-reduce(f32[2304]{0:T(1024)S(1)} %fusion.1), channel_id=1, replica_groups=mesh['ka'=64,'row'=8] {'ka'}, use_global_device_ids=true, to_apply=%region_1.0 | all-reduce | flops 2304 | bytes 18432 | tf_op jit(solution)/shard_map/pmax | solution.py:19
  241.4 0.0 copy-done
  241.4 11.4 %convolution_bitcast_fusion = f32[256,2304]{0,1:T(8,128)} fusion(bf16[256,256]{1,0:T(8,128)(2,1)S(1)} %copy-done, bf16[2304,256]{1,0:T(8,128)(2,1)} %param.4, f32[2304]{0:T(1024)S(1)} %get-tuple-element.10, f32[2304]{0:T(1024)S(1)} %get-tuple-element.9), kind=kOutput, calls=%fused_computation.1 | convolution fusion | flops 305528832 | bytes 3688448 | tf_op jit(solution)/shard_map/dot_general | solution.py:22
  252.7 1.3 dynamic-slice
  254.7 0.0 copy-start.1
  254.7 245.4 %all-reduce.2 = bf16[256,2304]{0,1:T(8,128)(2,1)S(1)} all-reduce(f32[256,2304]{0,1:T(8,128)} %convolution_bitcast_fusion), channel_id=2, replica_groups=mesh['ka'=64,'row'=8] {'ka'}, use_global_device_ids=true, to_apply=%region_2.0.clone | all-reduce | flops 589824 | bytes 3538944
  500.1 0.0 all-gather.3.cloned.1.call-done
  500.1 3.1 reshape.10
  503.2 0.0 copy-done.1
  503.2 12.6 %convolution_bitcast_fusion.1 = f32[256,256]{0,1:T(8,128)S(1)} fusion(bf16[256,2304]{1,0:T(8,128)(2,1)} %reshape.10, bf16[2304,256]{1,0:T(8,128)(2,1)S(1)} %copy-done.1, f32[2304]{0:T(1024)S(1)} %get-tuple-element.10, f32[2304]{0:T(1024)S(1)} %get-tuple-element.9), kind=kOutput, calls=%fused_computation.12 | convolution fusion | flops 305528832 | bytes 2639872 | tf_op jit(solution)/shard_map/dot_general | solution.py:30
  515.9 0.0 copy-start.2
  515.9 0.8 copy.12
  516.7 0.0 reduce-scatter.5.cloned.1.call-update
  516.7 0.2 dynamic-slice_convert_fusion
  517.0 0.9 copy.8
  517.8 0.0 copy-done.2
  517.8 1.5 fusion
  519.4 135.9 %reduce-scatter.5.cloned.1.call-done = f32[32,256]{1,0:T(8,128)} async-done(((f32[256,256]{1,0:T(8,128)}), f32[32,256]{1,0:T(8,128)}) %reduce-scatter.5.cloned.1.call-update) | async-done | bytes 32784
  655.3 0.9 copy.13
  656.2 0.7 copy.9
  (1 shorter events, 0.0 us)
Async XLA Ops:
  7.2 234.2 %copy-start = (bf16[256,256]{1,0:T(8,128)(2,1)S(1)}, bf16[256,256]{1,0:T(8,128)(2,1)}, u32[]{:S(2)}) copy-start(bf16[256,256]{1,0:T(8,128)(2,1)} %param.3) | copy-start | bytes 393220
  7.2 492.9 %all-gather.3.cloned.1.call-start = ((), (), s32[]{:S(2)}) async-start(), calls=%async_computation.1 | async-start | bytes 1198080 | tf_op jit(solution)/shard_map/all_gather | solution.py:29
  7.9 647.4 %reduce-scatter.5.cloned.1.call-start = ((), (), s32[]{:S(2)}) async-start(), calls=%async_computation.2 | async-start | bytes 294912
  254.7 248.6 %copy-start.1 = (bf16[2304,256]{1,0:T(8,128)(2,1)S(1)}, bf16[2304,256]{1,0:T(8,128)(2,1)}, u32[]{:S(2)}) copy-start(bf16[2304,256]{1,0:T(8,128)(2,1)} %param.4) | copy-start | bytes 3538948
  515.9 2.0 copy-start.2
Sparse Core Ops, SparseCore 0:
  11.0 135.3 all-gather.2
  516.9 138.3 reduce-scatter.4
where the time goes:
time: 665 us; the launch traced here: 664 us
  blocking collectives  477 us (72%)
  waiting for transfers between devices  137 us (21%)
  matrix products  25.6 us (4%)
  between operations  14.8 us (2%)
  local copies, waits for them, and re-layouts  7.86 us (1%)
    unnamed x1, blocking collectives  245 us
    pmax x1, blocking collectives, local(): peak = lax.pmax(jnp.max(jnp.abs(wide), axis=1), 'ka')  232 us
    unnamed x3, waiting for transfers between devices  137 us
  transfers between devices with their start and end apart: 2, of which 1 were waited for; matrix products, arithmetic and copies ran while one was open for 3% of the time, Pallas kernels for 0%

commit v1 on v0

v1 whole, which is shorter than its diff:
```python
import functools
import math

import jax
import jax.numpy as jnp
import numpy as np
from jax import lax
from jax.experimental import pallas as pl
from jax.experimental.pallas import tpu as pltpu
from jax.sharding import PartitionSpec as P

LEVELS = 7
MESH = pl.DeviceIdType.MESH
F32 = jnp.float32
BF16 = jnp.bfloat16

Z, Y, TOK = 16, 4, 4
CLASS = Z // 4
ROWS = 8
PIECES = (256, 512, 768, 768)

WINDOW = [(dy, dz) for dz in (2, 1, -1, 0) for dy in range(Y) if (dy, dz) != (0, 0)]
FAR = (8, 4, 12)
NEAR = (2, 1, 15)
AROUND = (8, 7, 9, 6, 10, 5, 11, 4, 12, 3, 13, 2, 14, 1, 15)


def sine_terms():
    nodes = 0.5 * np.cos((np.arange(4000) + 0.5) * np.pi / 8000)
    t = nodes * nodes
    basis = np.stack([t**k for k in range(7)], axis=1)
    scale = nodes[:, None]
    terms, *_ = np.linalg.lstsq(basis * scale, np.sin(2 * np.pi * nodes), rcond=None)
    return [float(c) for c in terms]


def quantized_block(wide, inverse, share, terms):
    turns = wide * inverse
    rest = turns - jnp.round(turns)
    square = rest * rest
    value = terms[-1] * square + terms[-2]
    for term in terms[-3::-1]:
        value = value * square + term
    return (wide - share * (rest * value)).astype(BF16)


def kernel(
    x_ref, w_ref, g_ref, projected_ref, input_ref, weight_ref,
    wt, qt, gathered, x_by_y, x_by_class, peak_own, peak_near, peak_mid, peak_far,
    part, part_in, sums, sums_in, grad, grad_in,
    near_s, near_r, far_s, far_r, g1_s, g1_r, g2_s, g2_r, g3_s, g3_r,
    part_s, part_r, sums_s, sums_r, grad_s, grad_r,
):
    ka, row = lax.axis_index("ka"), lax.axis_index("row")
    z, y = ka // Y, ka % Y
    low, high = z % 4, z // 4
    columns = w_ref.shape[0]
    terms = sine_terms()

    def at(dz, dy):
        return (lax.rem(z + dz + Z, Z) * Y + lax.rem(y + dy, Y), row)

    def beside(d):
        return (ka, lax.rem(row + d, ROWS))

    def send(source, target, sent, arrived, device):
        copy = pltpu.make_async_remote_copy(
            src_ref=source, dst_ref=target, send_sem=sent, recv_sem=arrived,
            device_id=device, device_id_type=MESH,
        )
        copy.start()
        return copy

    barrier = pltpu.get_barrier_semaphore()
    greeted = [at(dz, 0) for dz in AROUND if dz not in (1, 2, 15)]
    greeted += [at(-dz, dy) for dy, dz in WINDOW] + [beside(d) for d in range(1, ROWS)]
    for device in greeted:
        pl.semaphore_signal(barrier, inc=1, device_id=device, device_id_type=MESH)

    for c in range(0, columns, 256):
        wt[:, c : c + 256] = w_ref[c : c + 256, :].T
    peak_own[...] = jnp.max(jnp.abs(wt[...].astype(F32)), axis=0, keepdims=True)
    slot = low * 16 + high * Y + y
    gathered[slot] = g_ref[...]

    pl.semaphore_wait(barrier, len(greeted))

    near = [
        send(peak_own, peak_near.at[i], near_s.at[i], near_r.at[i], at(dz, dy))
        for i, (dy, dz) in enumerate(WINDOW)
    ]
    gather1 = [
        send(gathered.at[slot], gathered.at[slot], g1_s.at[i], g1_r.at[i], at(dz, 0))
        for i, dz in enumerate(FAR)
    ]

    to = lax.broadcasted_iota(jnp.int32, (256, 256), 0)
    come = lax.broadcasted_iota(jnp.int32, (256, 256), 1)
    order = jnp.where(come == to % 64 // TOK * 16 + to // 64 * TOK + to % TOK, 1.0, 0.0)
    x_by_y[...] = jnp.dot(order.astype(BF16), x_ref[...], preferred_element_type=F32).astype(BF16)
    for zh in range(4):
        for zl in range(4):
            x_by_class[64 * zl + 16 * zh : 64 * zl + 16 * zh + 16, :] = x_ref[
                64 * zh + 16 * zl : 64 * zh + 16 * zl + 16, :
            ]

    peak = peak_own[...]
    for i, copy in enumerate(near):
        copy.wait_recv()
        peak = jnp.maximum(peak, peak_near[i])
    peak_mid[...] = peak
    far = [
        send(peak_mid, peak_far.at[i], far_s.at[i], far_r.at[i], at(dz, 0))
        for i, dz in enumerate(FAR)
    ]

    for copy in gather1:
        copy.wait_recv()
    gather2 = []
    for dy in (2, 1, 3):
        for zh in range(4):
            i = len(gather2)
            held = gathered.at[low * 16 + zh * Y + y]
            gather2.append(send(held, held, g2_s.at[i], g2_r.at[i], at(0, dy)))

    for i, copy in enumerate(far):
        copy.wait_recv()
        peak = jnp.maximum(peak, peak_far[i])
    inverse = LEVELS / peak
    share = peak * (1.0 / (LEVELS * 2.0 * math.pi))

    starts = [sum(PIECES[:p]) for p in range(len(PIECES))]
    spans = [slice(s, s + n) for s, n in zip(starts, PIECES)]
    by_y, gather3 = [], []
    for p, span in enumerate(spans):
        for c in range(span.start, span.stop, 256):
            block = slice(c, c + 256)
            qt[:, block] = quantized_block(
                wt[:, block].astype(F32), inverse[:, block], share[:, block], terms
            )
            product = jnp.dot(x_by_y[...], qt[:, block], preferred_element_type=F32)
            part[:, :, block] = product.astype(BF16).reshape(Y, 64, 256)
        cut = pl.ds(span.start, PIECES[p])
        by_y.append([
            send(
                part.at[lax.rem(y + dy, Y), :, cut], part_in.at[i, :, cut],
                part_s.at[p, i], part_r.at[p, i], at(0, dy),
            )
            for i, dy in enumerate((2, 1, 3))
        ])
        if p == 0:
            for copy in gather2:
                copy.wait_recv()
            held = gathered.at[pl.ds(low * 16, 16)]
            gather3 = [
                send(held, held, g3_s.at[i], g3_r.at[i], at(dz, 0)) for i, dz in enumerate(NEAR)
            ]

    by_z = []
    for p, span in enumerate(spans):
        for copy in by_y[p]:
            copy.wait_recv()
        total = part[y, :, span].astype(F32)
        for i in range(3):
            total += part_in[i, :, span].astype(F32)
        for k in range(Z):
            sums[k, :, span] = total[TOK * k : TOK * k + TOK, :].astype(BF16)
        cut = pl.ds(span.start, PIECES[p])
        by_z.append([
            send(
                sums.at[lax.rem(z + dz, Z), :, cut], sums_in.at[i, :, cut],
                sums_s.at[p, i], sums_r.at[p, i], at(dz, 0),
            )
            for i, dz in enumerate(AROUND)
        ])

    for copy in gather3:
        copy.wait_recv()
    tokens = gathered[...].reshape(256, columns)
    product = lax.dot_general(
        tokens, qt[...], (((1,), (1,)), ((), ())), preferred_element_type=F32
    )
    for k in range(Z):
        start = 64 * (k % 4) + 16 * (k // 4)
        grad[k // 2, 16 * (k % 2) : 16 * (k % 2) + 16, :] = product[start : start + 16, :]
    by_row = [
        send(
            grad.at[lax.rem(row + d, ROWS)], grad_in.at[d - 1],
            grad_s.at[d - 1], grad_r.at[d - 1], beside(d),
        )
        for d in range(1, ROWS)
    ]

    for c in range(0, columns, 256):
        block = gathered[:, :, c : c + 256].reshape(256, 256)
        product = lax.dot_general(
            block, x_by_class[...], (((0,), (0,)), ((), ())), preferred_element_type=F32
        )
        weight_ref[c : c + 256, :] = (product * (1.0 / math.sqrt(x_ref.shape[0]))).astype(BF16)

    total = grad[row]
    for i, copy in enumerate(by_row):
        copy.wait_recv()
        total += grad_in[i]
    input_ref[...] = total.astype(BF16)

    for p, span in enumerate(spans):
        total = sums[z, :, span].astype(F32)
        for i, copy in enumerate(by_z[p]):
            copy.wait_recv()
            total += sums_in[i, :, span].astype(F32)
        projected_ref[:, span] = total.astype(BF16)

    for copy in near + far + gather1 + gather2 + gather3 + by_row + sum(by_y, []) + sum(by_z, []):
        copy.wait_send()


def local(inputs, weight, out_grad):
    columns, depth = weight.shape
    pieces = len(PIECES)
    whole = pl.BlockSpec(memory_space=pltpu.VMEM)
    dma = pltpu.SemaphoreType.DMA
    return pl.pallas_call(
        kernel,
        out_shape=(
            jax.ShapeDtypeStruct(out_grad.shape, BF16),
            jax.ShapeDtypeStruct((inputs.shape[0] // ROWS, depth), BF16),
            jax.ShapeDtypeStruct(weight.shape, BF16),
        ),
        in_specs=[whole] * 3,
        out_specs=(whole,) * 3,
        scratch_shapes=[
            pltpu.VMEM((depth, columns), BF16),
            pltpu.VMEM((depth, columns), BF16),
            pltpu.VMEM((Y * Z, TOK, columns), BF16),
            pltpu.VMEM(inputs.shape, BF16),
            pltpu.VMEM(inputs.shape, BF16),
            pltpu.VMEM((1, columns), F32),
            pltpu.VMEM((len(WINDOW), 1, columns), F32),
            pltpu.VMEM((1, columns), F32),
            pltpu.VMEM((len(FAR), 1, columns), F32),
            pltpu.VMEM((Y, Z * TOK, columns), BF16),
            pltpu.VMEM((Y - 1, Z * TOK, columns), BF16),
            pltpu.VMEM((Z, TOK, columns), BF16),
            pltpu.VMEM((Z - 1, TOK, columns), BF16),
            pltpu.VMEM((ROWS, inputs.shape[0] // ROWS, depth), F32),
            pltpu.VMEM((ROWS - 1, inputs.shape[0] // ROWS, depth), F32),
            dma((len(WINDOW),)), dma((len(WINDOW),)), dma((len(FAR),)), dma((len(FAR),)),
            dma((len(FAR),)), dma((len(FAR),)), dma((12,)), dma((12,)),
            dma((len(NEAR),)), dma((len(NEAR),)),
            dma((pieces, Y - 1)), dma((pieces, Y - 1)), dma((pieces, Z - 1)), dma((pieces, Z - 1)),
            dma((ROWS - 1,)), dma((ROWS - 1,)),
        ],
        compiler_params=pltpu.CompilerParams(
            collective_id=0, has_side_effects=True, vmem_limit_bytes=48 * 2**20
        ),
        name="joined_projection",
    )(inputs, weight, out_grad)


def solution(mesh):
    placed = (P(None, "ka"), P("row", "ka"), P("ka", "row"))
    return jax.shard_map(
        local,
        mesh=mesh,
        in_specs=placed,
        out_specs=(P("ka", "row"), P("row", "ka"), P("row", "ka")),
        check_vma=False,
    )
```

time: 665 us -> 73.3 us (0.11)
  the two profiles are of different devices: /device:TPU:1 before, /device:TPU:2 now
where the time goes in v1:
time: 73.3 us; the launch traced here: 73.1 us
  Pallas kernels  67.3 us (92%)
  local copies, waits for them, and re-layouts  5.11 us (7%)
    pallas_call x1, Pallas kernels, local(): pl.pallas_call(kernel, out_shape=(jax.ShapeDtypeStruct(out_grad.shape, BF...  67.3 us
    unnamed x9, local copies, waits for them, and re-layouts  5.11 us

profile of v1, /device:TPU:2, one launch (start us, length us, event | category | flops | bytes accessed | tf_op | source)
XLA Modules:
  0.0 73.1 jit_solution(1570056190720021860)
XLA Ops:
  0.6 0.0 copy-start
  0.6 1.3 %copy-done = bf16[2304,256]{1,0:T(8,128)(2,1)S(1)} copy-done((bf16[2304,256]{1,0:T(8,128)(2,1)S(1)}, bf16[2304,256]{1,0:T(8,128)(2,1)}, u32[]{:S(2)}) %copy-start) | copy-done | bytes 1179672
  1.9 0.0 copy-start.1
  1.9 0.9 %copy-done.1 = bf16[256,256]{1,0:T(8,128)(2,1)S(1)} copy-done((bf16[256,256]{1,0:T(8,128)(2,1)S(1)}, bf16[256,256]{1,0:T(8,128)(2,1)}, u32[]{:S(2)}) %copy-start.1) | copy-done | bytes 131096
  2.8 0.0 copy-start.2
  2.8 0.7 copy-done.2
  3.5 67.3 %joined_projection.1 = (bf16[4,2304]{1,0:T(4,128)(2,1)S(1)}, bf16[32,256]{1,0:T(8,128)(2,1)S(1)}, bf16[2304,256]{1,0:T(8,128)(2,1)S(1)}) custom-call(bf16[256,256]{1,0:T(8,128)(2,1)S(1)} %copy-done.1, bf16[2304,256]{1,0:T(8,128)(2,1)S(1)} %copy-done, bf16[4,2304]{1,0:T(4,128)(2,1)S(1)} %copy-done.2), custom_call_target="tpu_custom_call" | custom-call | tf_op jit(solution)/shard_map/joined_projection/pallas_call | solution.py:223
  70.8 0.6 copy.9
  71.4 0.6 copy.10
  72.0 1.0 %copy.11 = bf16[2304,256]{1,0:T(8,128)(2,1)} copy(bf16[2304,256]{1,0:T(8,128)(2,1)S(1)} %get-tuple-element.8) | data formatting | bytes 2359296
Async XLA Ops:
  0.6 1.3 %copy-start = (bf16[2304,256]{1,0:T(8,128)(2,1)S(1)}, bf16[2304,256]{1,0:T(8,128)(2,1)}, u32[]{:S(2)}) copy-start(bf16[2304,256]{1,0:T(8,128)(2,1)} %w_ref.1) | copy-start | bytes 3538948
  1.9 0.9 %copy-start.1 = (bf16[256,256]{1,0:T(8,128)(2,1)S(1)}, bf16[256,256]{1,0:T(8,128)(2,1)}, u32[]{:S(2)}) copy-start(bf16[256,256]{1,0:T(8,128)(2,1)} %x_ref.1) | copy-start | bytes 393220
  2.8 0.7 copy-start.2

commit v2 on v1

--- a/solution.py
+++ b/solution.py
@@ -17,7 +17,8 @@
 Z, Y, TOK = 16, 4, 4
 CLASS = Z // 4
 ROWS = 8
-PIECES = (256, 512, 768, 768)
+PIECES = (256, 512, 512, 512, 256, 256)
+DIRECT = 2
 
 WINDOW = [(dy, dz) for dz in (2, 1, -1, 0) for dy in range(Y) if (dy, dz) != (0, 0)]
 FAR = (8, 4, 12)
@@ -45,16 +46,16 @@
 
 
 def kernel(
-    x_ref, w_ref, g_ref, projected_ref, input_ref, weight_ref,
-    wt, qt, gathered, x_by_y, x_by_class, peak_own, peak_near, peak_mid, peak_far,
-    part, part_in, sums, sums_in, grad, grad_in,
+    x_hbm, w_hbm, g_hbm, projected_ref, input_ref, weight_ref,
+    x_ref, w_ref, g_ref, load_sem, wt, qt, gathered, x_by_y, x_by_class, peak_own, peak_near, peak_mid, peak_far,
+    part, part_in, sums, near_in, sums_far, sums_in, grad, grad_in,
     near_s, near_r, far_s, far_r, g1_s, g1_r, g2_s, g2_r, g3_s, g3_r,
-    part_s, part_r, sums_s, sums_r, grad_s, grad_r,
+    part_s, part_r, part_near_s, part_near_r, sums_s, sums_r, grad_s, grad_r,
 ):
     ka, row = lax.axis_index("ka"), lax.axis_index("row")
     z, y = ka // Y, ka % Y
     low, high = z % 4, z // 4
-    columns = w_ref.shape[0]
+    columns = w_hbm.shape[0]
     terms = sine_terms()
 
     def at(dz, dy):
@@ -77,10 +78,20 @@
     for device in greeted:
         pl.semaphore_signal(barrier, inc=1, device_id=device, device_id_type=MESH)
 
+    loads = [
+        pltpu.make_async_copy(source, target, load_sem.at[i])
+        for i, (source, target) in enumerate(((w_hbm, w_ref), (g_hbm, g_ref), (x_hbm, x_ref)))
+    ]
+    for copy in loads:
+        copy.start()
+
+    loads[0].wait()
     for c in range(0, columns, 256):
         wt[:, c : c + 256] = w_ref[c : c + 256, :].T
     peak_own[...] = jnp.max(jnp.abs(wt[...].astype(F32)), axis=0, keepdims=True)
-    slot = low * 16 + high * Y + y
+    slot = low * 16 + y * CLASS + high
+    loads[1].wait()
+    loads[2].wait()
     gathered[slot] = g_ref[...]
 
     pl.semaphore_wait(barrier, len(greeted))
@@ -96,13 +107,11 @@
 
     to = lax.broadcasted_iota(jnp.int32, (256, 256), 0)
     come = lax.broadcasted_iota(jnp.int32, (256, 256), 1)
-    order = jnp.where(come == to % 64 // TOK * 16 + to // 64 * TOK + to % TOK, 1.0, 0.0)
-    x_by_y[...] = jnp.dot(order.astype(BF16), x_ref[...], preferred_element_type=F32).astype(BF16)
-    for zh in range(4):
-        for zl in range(4):
-            x_by_class[64 * zl + 16 * zh : 64 * zl + 16 * zh + 16, :] = x_ref[
-                64 * zh + 16 * zl : 64 * zh + 16 * zl + 16, :
-            ]
+    by_y = to % 64 // TOK * 16 + to // 64 * TOK + to % TOK
+    by_class = to // 64 * 16 + to // 16 % 4 * TOK + to // 4 % 4 * 64 + to % TOK
+    for source, target in ((by_y, x_by_y), (by_class, x_by_class)):
+        order = jnp.where(come == source, 1.0, 0.0).astype(BF16)
+        target[...] = jnp.dot(order, x_ref[...], preferred_element_type=F32).astype(BF16)
 
     peak = peak_own[...]
     for i, copy in enumerate(near):
@@ -116,12 +125,11 @@
 
     for copy in gather1:
         copy.wait_recv()
-    gather2 = []
-    for dy in (2, 1, 3):
-        for zh in range(4):
-            i = len(gather2)
-            held = gathered.at[low * 16 + zh * Y + y]
-            gather2.append(send(held, held, g2_s.at[i], g2_r.at[i], at(0, dy)))
+    held = gathered.at[pl.ds(low * 16 + y * CLASS, CLASS)]
+    gather2 = [
+        send(held, held, g2_s.at[i], g2_r.at[i], device)
+        for i, device in enumerate([at(dz, 0) for dz in NEAR] + [at(0, dy) for dy in (2, 1, 3)])
+    ]
 
     for i, copy in enumerate(far):
         copy.wait_recv()
@@ -151,12 +159,33 @@
         if p == 0:
             for copy in gather2:
                 copy.wait_recv()
-            held = gathered.at[pl.ds(low * 16, 16)]
-            gather3 = [
-                send(held, held, g3_s.at[i], g3_r.at[i], at(dz, 0)) for i, dz in enumerate(NEAR)
-            ]
-
-    by_z = []
+            for dy in (2, 1, 3):
+                first = low * 16 + lax.rem(y + dy, Y) * CLASS
+                for dz, start, size in ((1, 0, 4), (15, 0, 4), (2, 0, 2), (14, 2, 2)):
+                    i = len(gather3)
+                    held = gathered.at[pl.ds(first + start, size)]
+                    gather3.append(send(held, held, g3_s.at[i], g3_r.at[i], at(dz, 0)))
+
+    def chunk(k):
+        return lax.rem(k, 4) * CLASS + k // 4
+
+    def near_total(p):
+        span, cut = spans[p], pl.ds(spans[p].start, PIECES[p])
+        for copy in by_near[p]:
+            copy.wait_recv()
+        total = sums[pl.ds(low * CLASS, CLASS), :, span].astype(F32)
+        for i in range(3):
+            total += near_in[i, :, :, span].astype(F32)
+        sums_far[:, :, span] = total.astype(BF16)
+        by_z[p] = [
+            send(
+                sums_far.at[lax.rem(high + m, CLASS), :, cut], sums_in.at[i, :, cut],
+                sums_s.at[p, i], sums_r.at[p, i], at(4 * m, 0),
+            )
+            for i, m in enumerate((2, 1, 3))
+        ]
+
+    by_z, by_near = {}, {}
     for p, span in enumerate(spans):
         for copy in by_y[p]:
             copy.wait_recv()
@@ -164,15 +193,31 @@
         for i in range(3):
             total += part_in[i, :, span].astype(F32)
         for k in range(Z):
-            sums[k, :, span] = total[TOK * k : TOK * k + TOK, :].astype(BF16)
+            sums[k % 4 * CLASS + k // 4, :, span] = total[TOK * k : TOK * k + TOK, :].astype(BF16)
         cut = pl.ds(span.start, PIECES[p])
-        by_z.append([
-            send(
-                sums.at[lax.rem(z + dz, Z), :, cut], sums_in.at[i, :, cut],
-                sums_s.at[p, i], sums_r.at[p, i], at(dz, 0),
-            )
-            for i, dz in enumerate(AROUND)
-        ])
+        if p >= len(PIECES) - DIRECT:
+            by_z[p] = [
+                send(
+                    sums.at[chunk(lax.rem(z + dz, Z)), :, cut], sums_in.at[i, :, cut],
+                    sums_s.at[p, i], sums_r.at[p, i], at(dz, 0),
+                )
+                for i, dz in enumerate(AROUND)
+            ]
+        else:
+            by_near[p] = [
+                send(
+                    sums.at[pl.ds(lax.rem(low + dz, 4) * CLASS + first, count), :, cut],
+                    near_in.at[i, pl.ds(first, count), :, cut],
+                    part_near_s.at[p, j], part_near_r.at[p, j], at(dz, 0),
+                )
+                for j, (i, dz, first, count) in enumerate(
+                    ((0, 1, 0, 4), (1, 15, 0, 4), (2, 2, 0, 2), (2, 14, 2, 2))
+                )
+            ]
+        if p >= 1 and p - 1 in by_near:
+            near_total(p - 1)
+    if not DIRECT:
+        near_total(len(PIECES) - 1)
 
     for copy in gather3:
         copy.wait_recv()
@@ -180,9 +225,9 @@
     product = lax.dot_general(
         tokens, qt[...], (((1,), (1,)), ((), ())), preferred_element_type=F32
     )
-    for k in range(Z):
-        start = 64 * (k % 4) + 16 * (k // 4)
-        grad[k // 2, 16 * (k % 2) : 16 * (k % 2) + 16, :] = product[start : start + 16, :]
+    for k in range(Y * Z):
+        start = k // Y % 4 * 64 + k % Y * 16 + k // 16 * TOK
+        grad[k // 8, k % 8 * TOK : k % 8 * TOK + TOK, :] = product[start : start + TOK, :]
     by_row = [
         send(
             grad.at[lax.rem(row + d, ROWS)], grad_in.at[d - 1],
@@ -196,7 +241,7 @@
         product = lax.dot_general(
             block, x_by_class[...], (((0,), (0,)), ((), ())), preferred_element_type=F32
         )
-        weight_ref[c : c + 256, :] = (product * (1.0 / math.sqrt(x_ref.shape[0]))).astype(BF16)
+        weight_ref[c : c + 256, :] = (product * (1.0 / math.sqrt(x_hbm.shape[0]))).astype(BF16)
 
     total = grad[row]
     for i, copy in enumerate(by_row):
@@ -205,13 +250,16 @@
     input_ref[...] = total.astype(BF16)
 
     for p, span in enumerate(spans):
-        total = sums[z, :, span].astype(F32)
+        direct = p >= len(PIECES) - DIRECT
+        total = (sums[chunk(z), :, span] if direct else sums_far[high, :, span]).astype(F32)
         for i, copy in enumerate(by_z[p]):
             copy.wait_recv()
             total += sums_in[i, :, span].astype(F32)
         projected_ref[:, span] = total.astype(BF16)
 
-    for copy in near + far + gather1 + gather2 + gather3 + by_row + sum(by_y, []) + sum(by_z, []):
+    for copy in near + far + gather1 + gather2 + gather3 + by_row + sum(by_y, []):
+        copy.wait_send()
+    for copy in sum(by_near.values(), []) + sum(by_z.values(), []):
         copy.wait_send()
 
 
@@ -227,9 +275,13 @@
             jax.ShapeDtypeStruct((inputs.shape[0] // ROWS, depth), BF16),
             jax.ShapeDtypeStruct(weight.shape, BF16),
         ),
-        in_specs=[whole] * 3,
+        in_specs=[pl.BlockSpec(memory_space=pltpu.HBM)] * 3,
         out_specs=(whole,) * 3,
         scratch_shapes=[
+            pltpu.VMEM(inputs.shape, BF16),
+            pltpu.VMEM(weight.shape, BF16),
+            pltpu.VMEM(out_grad.shape, BF16),
+            dma((3,)),
             pltpu.VMEM((depth, columns), BF16),
             pltpu.VMEM((depth, columns), BF16),
             pltpu.VMEM((Y * Z, TOK, columns), BF16),
@@ -242,17 +294,19 @@
             pltpu.VMEM((Y, Z * TOK, columns), BF16),
             pltpu.VMEM((Y - 1, Z * TOK, columns), BF16),
             pltpu.VMEM((Z, TOK, columns), BF16),
+            pltpu.VMEM((3, CLASS, TOK, columns), BF16),
+            pltpu.VMEM((CLASS, TOK, columns), BF16),
             pltpu.VMEM((Z - 1, TOK, columns), BF16),
             pltpu.VMEM((ROWS, inputs.shape[0] // ROWS, depth), F32),
             pltpu.VMEM((ROWS - 1, inputs.shape[0] // ROWS, depth), F32),
             dma((len(WINDOW),)), dma((len(WINDOW),)), dma((len(FAR),)), dma((len(FAR),)),
-            dma((len(FAR),)), dma((len(FAR),)), dma((12,)), dma((12,)),
-            dma((len(NEAR),)), dma((len(NEAR),)),
-            dma((pieces, Y - 1)), dma((pieces, Y - 1)), dma((pieces, Z - 1)), dma((pieces, Z - 1)),
+            dma((len(FAR),)), dma((len(FAR),)), dma((6,)), dma((6,)), dma((12,)), dma((12,)),
+            dma((pieces, Y - 1)), dma((pieces, Y - 1)), dma((pieces, 4)), dma((pieces, 4)),
+            dma((pieces, Z - 1)), dma((pieces, Z - 1)),
             dma((ROWS - 1,)), dma((ROWS - 1,)),
         ],
         compiler_params=pltpu.CompilerParams(
-            collective_id=0, has_side_effects=True, vmem_limit_bytes=48 * 2**20
+            collective_id=0, has_side_effects=True, vmem_limit_bytes=int(52.4 * 2**20)
         ),
         name="joined_projection",
     )(inputs, weight, out_grad)

time: 73.3 us -> 64.3 us (0.88)
  the two profiles are of different devices: /device:TPU:2 before, /device:TPU:1 now
where the time goes in v2:
time: 64.3 us; the launch traced here: 64.1 us
  Pallas kernels  59.6 us (93%)
  local copies, waits for them, and re-layouts  3.84 us (6%)
  between operations  0.65 us (1%)
    pallas_call x1, Pallas kernels, local(): pl.pallas_call(kernel, out_shape=(jax.ShapeDtypeStruct(out_grad.shape, BF...  59.6 us
    unnamed x7, local copies, waits for them, and re-layouts  3.84 us

profile of v2, /device:TPU:1, one launch (start us, length us, event | category | flops | bytes accessed | tf_op | source)
XLA Modules:
  0.0 64.1 jit_solution(9042846581267318008)
XLA Ops:
  0.6 0.0 copy-start
  0.6 0.9 %copy-done = bf16[256,256]{1,0:T(8,128)(2,1)S(1)} copy-done((bf16[256,256]{1,0:T(8,128)(2,1)S(1)}, bf16[256,256]{1,0:T(8,128)(2,1)}, u32[]{:S(2)}) %copy-start) | copy-done | bytes 131096
  1.5 0.0 copy-start.1
  1.5 0.7 %copy-done.1 = bf16[4,2304]{1,0:T(4,128)(2,1)S(1)} copy-done((bf16[4,2304]{1,0:T(4,128)(2,1)S(1)}, bf16[4,2304]{1,0:T(4,128)(2,1)}, u32[]{:S(2)}) %copy-start.1) | copy-done | bytes 18456
  2.3 59.6 %joined_projection.1 = (bf16[4,2304]{1,0:T(4,128)(2,1)S(1)}, bf16[32,256]{1,0:T(8,128)(2,1)S(1)}, bf16[2304,256]{1,0:T(8,128)(2,1)S(1)}) custom-call(bf16[256,256]{1,0:T(8,128)(2,1)S(1)} %copy-done, bf16[2304,256]{1,0:T(8,128)(2,1)} %w_hbm.1, bf16[4,2304]{1,0:T(4,128)(2,1)S(1)} %copy-done.1), custom_call_target="tpu_custom_call" | custom-call | tf_op jit(solution)/shard_map/joined_projection/pallas_call | solution.py:271
  61.8 0.6 copy.9
  62.4 0.6 copy.10
  63.0 1.0 %copy.11 = bf16[2304,256]{1,0:T(8,128)(2,1)} copy(bf16[2304,256]{1,0:T(8,128)(2,1)S(1)} %get-tuple-element.8) | data formatting | bytes 2359296
Async XLA Ops:
  0.6 0.9 %copy-start = (bf16[256,256]{1,0:T(8,128)(2,1)S(1)}, bf16[256,256]{1,0:T(8,128)(2,1)}, u32[]{:S(2)}) copy-start(bf16[256,256]{1,0:T(8,128)(2,1)} %x_hbm.1) | copy-start | bytes 393220
  1.5 0.7 %copy-start.1 = (bf16[4,2304]{1,0:T(4,128)(2,1)S(1)}, bf16[4,2304]{1,0:T(4,128)(2,1)}, u32[]{:S(2)}) copy-start(bf16[4,2304]{1,0:T(4,128)(2,1)} %g_hbm.1) | copy-start | bytes 55300

commit v3 on v2

--- a/solution.py
+++ b/solution.py
@@ -18,7 +18,7 @@
 CLASS = Z // 4
 ROWS = 8
 PIECES = (256, 512, 512, 512, 256, 256)
-DIRECT = 2
+DIRECT = 4
 
 WINDOW = [(dy, dz) for dz in (2, 1, -1, 0) for dy in range(Y) if (dy, dz) != (0, 0)]
 FAR = (8, 4, 12)
@@ -46,8 +46,8 @@
 
 
 def kernel(
-    x_hbm, w_hbm, g_hbm, projected_ref, input_ref, weight_ref,
-    x_ref, w_ref, g_ref, load_sem, wt, qt, gathered, x_by_y, x_by_class, peak_own, peak_near, peak_mid, peak_far,
+    x_hbm, w_hbm, g_hbm, projected_hbm, input_hbm, weight_hbm,
+    projected_ref, input_ref, weight_ref, store_sem, x_ref, w_ref, g_ref, load_sem, wt, qt, gathered, x_by_y, x_by_class, peak_own, peak_near, peak_mid, peak_far,
     part, part_in, sums, near_in, sums_far, sums_in, grad, grad_in,
     near_s, near_r, far_s, far_r, g1_s, g1_r, g2_s, g2_r, g3_s, g3_r,
     part_s, part_r, part_near_s, part_near_r, sums_s, sums_r, grad_s, grad_r,
@@ -160,11 +160,17 @@
             for copy in gather2:
                 copy.wait_recv()
             for dy in (2, 1, 3):
-                first = low * 16 + lax.rem(y + dy, Y) * CLASS
-                for dz, start, size in ((1, 0, 4), (15, 0, 4), (2, 0, 2), (14, 2, 2)):
+                held_y = low * 16 + lax.rem(y + dy, Y) * CLASS
+                for dz, start, size in ((1, 0, 3), (15, 0, 3), (2, 0, 2), (14, 2, 1)):
                     i = len(gather3)
-                    held = gathered.at[pl.ds(first + start, size)]
+                    held = gathered.at[pl.ds(held_y + start, size)]
                     gather3.append(send(held, held, g3_s.at[i], g3_r.at[i], at(dz, 0)))
+
+    for dz in (1, 2, 3):
+        held = gathered.at[pl.ds(lax.rem(low + dz, 4) * 16 + y * CLASS + 3, 1)]
+        for dy in (2, 1, 3):
+            i = len(gather3)
+            gather3.append(send(held, held, g3_s.at[i], g3_r.at[i], at(0, dy)))
 
     def chunk(k):
         return lax.rem(k, 4) * CLASS + k // 4
@@ -243,11 +249,20 @@
         )
         weight_ref[c : c + 256, :] = (product * (1.0 / math.sqrt(x_hbm.shape[0]))).astype(BF16)
 
+    stores = [
+        pltpu.make_async_copy(source, target, store_sem.at[i])
+        for i, (source, target) in enumerate(
+            ((weight_ref, weight_hbm), (input_ref, input_hbm), (projected_ref, projected_hbm))
+        )
+    ]
+    stores[0].start()
+
     total = grad[row]
     for i, copy in enumerate(by_row):
         copy.wait_recv()
         total += grad_in[i]
     input_ref[...] = total.astype(BF16)
+    stores[1].start()
 
     for p, span in enumerate(spans):
         direct = p >= len(PIECES) - DIRECT
@@ -256,28 +271,56 @@
             copy.wait_recv()
             total += sums_in[i, :, span].astype(F32)
         projected_ref[:, span] = total.astype(BF16)
+    stores[2].start()
 
     for copy in near + far + gather1 + gather2 + gather3 + by_row + sum(by_y, []):
         copy.wait_send()
     for copy in sum(by_near.values(), []) + sum(by_z.values(), []):
         copy.wait_send()
+    for copy in stores:
+        copy.wait()
+
+
+def hand_over(*refs):
+    sources, targets, held, came, done = refs[:3], refs[3:6], refs[6:9], refs[9], refs[10]
+    moves = []
+    for source, target, here in zip(sources, targets, held):
+        rows = source.shape[0]
+        parts = 4 if rows >= 2048 else 1
+        for k in range(parts):
+            cut, i = pl.ds(k * (rows // parts), rows // parts), len(moves)
+            moves.append((
+                pltpu.make_async_copy(source.at[cut], here.at[cut], came.at[i]),
+                pltpu.make_async_copy(here.at[cut], target.at[cut], done.at[i]),
+            ))
+    for come, _ in moves:
+        come.start()
+    for come, go in moves:
+        come.wait()
+        go.start()
+    for _, go in moves:
+        go.wait()
 
 
 def local(inputs, weight, out_grad):
     columns, depth = weight.shape
     pieces = len(PIECES)
-    whole = pl.BlockSpec(memory_space=pltpu.VMEM)
+    anywhere = pl.BlockSpec(memory_space=pl.ANY)
     dma = pltpu.SemaphoreType.DMA
-    return pl.pallas_call(
+    results = pl.pallas_call(
         kernel,
         out_shape=(
             jax.ShapeDtypeStruct(out_grad.shape, BF16),
             jax.ShapeDtypeStruct((inputs.shape[0] // ROWS, depth), BF16),
             jax.ShapeDtypeStruct(weight.shape, BF16),
         ),
-        in_specs=[pl.BlockSpec(memory_space=pltpu.HBM)] * 3,
-        out_specs=(whole,) * 3,
+        in_specs=[anywhere] * 3,
+        out_specs=(anywhere,) * 3,
         scratch_shapes=[
+            pltpu.VMEM(out_grad.shape, BF16),
+            pltpu.VMEM((inputs.shape[0] // ROWS, depth), BF16),
+            pltpu.VMEM(weight.shape, BF16),
+            dma((3,)),
             pltpu.VMEM(inputs.shape, BF16),
             pltpu.VMEM(weight.shape, BF16),
             pltpu.VMEM(out_grad.shape, BF16),
@@ -300,16 +343,24 @@
             pltpu.VMEM((ROWS, inputs.shape[0] // ROWS, depth), F32),
             pltpu.VMEM((ROWS - 1, inputs.shape[0] // ROWS, depth), F32),
             dma((len(WINDOW),)), dma((len(WINDOW),)), dma((len(FAR),)), dma((len(FAR),)),
-            dma((len(FAR),)), dma((len(FAR),)), dma((6,)), dma((6,)), dma((12,)), dma((12,)),
+            dma((len(FAR),)), dma((len(FAR),)), dma((6,)), dma((6,)), dma((21,)), dma((21,)),
             dma((pieces, Y - 1)), dma((pieces, Y - 1)), dma((pieces, 4)), dma((pieces, 4)),
             dma((pieces, Z - 1)), dma((pieces, Z - 1)),
             dma((ROWS - 1,)), dma((ROWS - 1,)),
         ],
         compiler_params=pltpu.CompilerParams(
-            collective_id=0, has_side_effects=True, vmem_limit_bytes=int(52.4 * 2**20)
+            collective_id=0, has_side_effects=True, vmem_limit_bytes=56 * 2**20
         ),
         name="joined_projection",
     )(inputs, weight, out_grad)
+    return pl.pallas_call(
+        hand_over,
+        out_shape=tuple(jax.ShapeDtypeStruct(a.shape, a.dtype) for a in results),
+        in_specs=[anywhere] * 3,
+        out_specs=(anywhere,) * 3,
+        scratch_shapes=[pltpu.VMEM(a.shape, a.dtype) for a in results] + [dma((6,)), dma((6,))],
+        name="hand_over",
+    )(*results)
 
 
 def solution(mesh):

time: 64.3 us -> 61 us (0.949)
  local copies, waits for them, and re-layouts: 3.84 us -> 0 us
    unnamed x7 -> x0, local copies, waits for them, and re-layouts: 3.84 us -> none
    pallas_call x0 -> x1, Pallas kernels: none -> 2.11 us  [local(): pl.pallas_call(hand_over, out_shape=tuple((jax.ShapeDtypeStruct(a.shape,...]
    pallas_call x1, Pallas kernels: 59.6 us -> 58.1 us  [local(): pl.pallas_call(kernel, out_shape=(jax.ShapeDtypeStruct(out_grad.shape, BF...]
where the time goes in v3:
time: 61 us; the launch traced here: 60.8 us
  Pallas kernels  60.2 us (99%)
  between operations  0.64 us (1%)
    pallas_call x1, Pallas kernels, local(): pl.pallas_call(kernel, out_shape=(jax.ShapeDtypeStruct(out_grad.shape, BF...  58.1 us
    pallas_call x1, Pallas kernels, local(): pl.pallas_call(hand_over, out_shape=tuple((jax.ShapeDtypeStruct(a.shape,...  2.11 us

profile of v3, /device:TPU:1, one launch (start us, length us, event | category | flops | bytes accessed | tf_op | source)
XLA Modules:
  0.0 60.8 jit_solution(11903158718768403136)
XLA Ops:
  0.6 58.1 %joined_projection.1 = (bf16[4,2304]{1,0:T(4,128)(2,1)}, bf16[32,256]{1,0:T(8,128)(2,1)}, bf16[2304,256]{1,0:T(8,128)(2,1)}) custom-call(bf16[256,256]{1,0:T(8,128)(2,1)} %x_hbm.1, bf16[2304,256]{1,0:T(8,128)(2,1)} %w_hbm.1, bf16[4,2304]{1,0:T(4,128)(2,1)} %g_hbm.1), custom_call_target="tpu_custom_call" | custom-call | tf_op jit(solution)/shard_map/joined_projection/pallas_call | solution.py:310
  58.7 2.1 %hand_over.1 = (bf16[4,2304]{1,0:T(4,128)(2,1)}, bf16[32,256]{1,0:T(8,128)(2,1)}, bf16[2304,256]{1,0:T(8,128)(2,1)}) custom-call(bf16[4,2304]{1,0:T(4,128)(2,1)} %get-tuple-element.6.refs_0_, bf16[32,256]{1,0:T(8,128)(2,1)} %get-tuple-element.7.refs_1_, bf16[2304,256]{1,0:T(8,128)(2,1)} %get-tuple-element.8.refs_2_), custom_call_target="tpu_custom_call" | custom-call | tf_op jit(solution)/shard_map/hand_over/pallas_call | solution.py:356

commit v4 on v3

--- a/solution.py
+++ b/solution.py
@@ -88,7 +88,9 @@
     loads[0].wait()
     for c in range(0, columns, 256):
         wt[:, c : c + 256] = w_ref[c : c + 256, :].T
-    peak_own[...] = jnp.max(jnp.abs(wt[...].astype(F32)), axis=0, keepdims=True)
+    peak = jnp.max(jnp.abs(wt[...].astype(F32)), axis=0, keepdims=True)
+    peak = jnp.concatenate([peak[:, : columns // 2], peak[:, columns // 2 :]], axis=0)
+    peak_own[...] = peak.astype(BF16)
     slot = low * 16 + y * CLASS + high
     loads[1].wait()
     loads[2].wait()
@@ -113,11 +115,10 @@
         order = jnp.where(come == source, 1.0, 0.0).astype(BF16)
         target[...] = jnp.dot(order, x_ref[...], preferred_element_type=F32).astype(BF16)
 
-    peak = peak_own[...]
     for i, copy in enumerate(near):
         copy.wait_recv()
-        peak = jnp.maximum(peak, peak_near[i])
-    peak_mid[...] = peak
+        peak = jnp.maximum(peak, peak_near[i].astype(F32))
+    peak_mid[...] = peak.astype(BF16)
     far = [
         send(peak_mid, peak_far.at[i], far_s.at[i], far_r.at[i], at(dz, 0))
         for i, dz in enumerate(FAR)
@@ -133,7 +134,8 @@
 
     for i, copy in enumerate(far):
         copy.wait_recv()
-        peak = jnp.maximum(peak, peak_far[i])
+        peak = jnp.maximum(peak, peak_far[i].astype(F32))
+    peak = jnp.concatenate([peak[0:1], peak[1:2]], axis=1)
     inverse = LEVELS / peak
     share = peak * (1.0 / (LEVELS * 2.0 * math.pi))
 
@@ -165,12 +167,12 @@
                     i = len(gather3)
                     held = gathered.at[pl.ds(held_y + start, size)]
                     gather3.append(send(held, held, g3_s.at[i], g3_r.at[i], at(dz, 0)))
-
-    for dz in (1, 2, 3):
-        held = gathered.at[pl.ds(lax.rem(low + dz, 4) * 16 + y * CLASS + 3, 1)]
-        for dy in (2, 1, 3):
-            i = len(gather3)
-            gather3.append(send(held, held, g3_s.at[i], g3_r.at[i], at(0, dy)))
+        if p == 3:
+            for dz in (1, 2, 3):
+                held = gathered.at[pl.ds(lax.rem(low + dz, 4) * 16 + y * CLASS + 3, 1)]
+                for dy in (2, 1, 3):
+                    i = len(gather3)
+                    gather3.append(send(held, held, g3_s.at[i], g3_r.at[i], at(0, dy)))
 
     def chunk(k):
         return lax.rem(k, 4) * CLASS + k // 4
@@ -330,10 +332,10 @@
             pltpu.VMEM((Y * Z, TOK, columns), BF16),
             pltpu.VMEM(inputs.shape, BF16),
             pltpu.VMEM(inputs.shape, BF16),
-            pltpu.VMEM((1, columns), F32),
-            pltpu.VMEM((len(WINDOW), 1, columns), F32),
-            pltpu.VMEM((1, columns), F32),
-            pltpu.VMEM((len(FAR), 1, columns), F32),
+            pltpu.VMEM((2, columns // 2), BF16),
+            pltpu.VMEM((len(WINDOW), 2, columns // 2), BF16),
+            pltpu.VMEM((2, columns // 2), BF16),
+            pltpu.VMEM((len(FAR), 2, columns // 2), BF16),
             pltpu.VMEM((Y, Z * TOK, columns), BF16),
             pltpu.VMEM((Y - 1, Z * TOK, columns), BF16),
             pltpu.VMEM((Z, TOK, columns), BF16),

time: 61 us -> 60.2 us (0.987)
  Pallas kernels: 60.2 us -> 59.4 us
    pallas_call x1, Pallas kernels: 58.1 us -> 57.3 us  [local(): pl.pallas_call(kernel, out_shape=(jax.ShapeDtypeStruct(out_grad.shape, BF...]
where the time goes in v4:
time: 60.2 us; the launch traced here: 60 us
  Pallas kernels  59.4 us (99%)
  between operations  0.64 us (1%)
    pallas_call x1, Pallas kernels, local(): pl.pallas_call(kernel, out_shape=(jax.ShapeDtypeStruct(out_grad.shape, BF...  57.3 us
    pallas_call x1, Pallas kernels, local(): pl.pallas_call(hand_over, out_shape=tuple((jax.ShapeDtypeStruct(a.shape,...  2.11 us

profile of v4, /device:TPU:1, one launch (start us, length us, event | category | flops | bytes accessed | tf_op | source)
XLA Modules:
  0.0 60.0 jit_solution(579380022881528056)
XLA Ops:
  0.6 57.3 %joined_projection.1 = (bf16[4,2304]{1,0:T(4,128)(2,1)}, bf16[32,256]{1,0:T(8,128)(2,1)}, bf16[2304,256]{1,0:T(8,128)(2,1)}) custom-call(bf16[256,256]{1,0:T(8,128)(2,1)} %x_hbm.1, bf16[2304,256]{1,0:T(8,128)(2,1)} %w_hbm.1, bf16[4,2304]{1,0:T(4,128)(2,1)} %g_hbm.1), custom_call_target="tpu_custom_call" | custom-call | tf_op jit(solution)/shard_map/joined_projection/pallas_call | solution.py:312
  57.9 2.1 %hand_over.1 = (bf16[4,2304]{1,0:T(4,128)(2,1)}, bf16[32,256]{1,0:T(8,128)(2,1)}, bf16[2304,256]{1,0:T(8,128)(2,1)}) custom-call(bf16[4,2304]{1,0:T(4,128)(2,1)} %get-tuple-element.6.refs_0_, bf16[32,256]{1,0:T(8,128)(2,1)} %get-tuple-element.7.refs_1_, bf16[2304,256]{1,0:T(8,128)(2,1)} %get-tuple-element.8.refs_2_), custom_call_target="tpu_custom_call" | custom-call | tf_op jit(solution)/shard_map/hand_over/pallas_call | solution.py:358

commit v5 on v4

--- a/solution.py
+++ b/solution.py
@@ -17,7 +17,7 @@
 Z, Y, TOK = 16, 4, 4
 CLASS = Z // 4
 ROWS = 8
-PIECES = (256, 512, 512, 512, 256, 256)
+PIECES = (512, 512, 512, 256, 256, 256)
 DIRECT = 4
 
 WINDOW = [(dy, dz) for dz in (2, 1, -1, 0) for dy in range(Y) if (dy, dz) != (0, 0)]

time: 60.2 us -> 59.3 us (0.985)
  Pallas kernels: 59.4 us -> 58.5 us
    pallas_call x1, Pallas kernels: 57.3 us -> 56.4 us  [local(): pl.pallas_call(kernel, out_shape=(jax.ShapeDtypeStruct(out_grad.shape, BF...]
where the time goes in v5:
time: 59.3 us; the launch traced here: 59.2 us
  Pallas kernels  58.5 us (99%)
  between operations  0.64 us (1%)
    pallas_call x1, Pallas kernels, local(): pl.pallas_call(kernel, out_shape=(jax.ShapeDtypeStruct(out_grad.shape, BF...  56.4 us
    pallas_call x1, Pallas kernels, local(): pl.pallas_call(hand_over, out_shape=tuple((jax.ShapeDtypeStruct(a.shape,...  2.11 us

profile of v5, /device:TPU:1, one launch (start us, length us, event | category | flops | bytes accessed | tf_op | source)
XLA Modules:
  0.0 59.2 jit_solution(6281458127637576546)
XLA Ops:
  0.6 56.4 %joined_projection.1 = (bf16[4,2304]{1,0:T(4,128)(2,1)}, bf16[32,256]{1,0:T(8,128)(2,1)}, bf16[2304,256]{1,0:T(8,128)(2,1)}) custom-call(bf16[256,256]{1,0:T(8,128)(2,1)} %x_hbm.1, bf16[2304,256]{1,0:T(8,128)(2,1)} %w_hbm.1, bf16[4,2304]{1,0:T(4,128)(2,1)} %g_hbm.1), custom_call_target="tpu_custom_call" | custom-call | tf_op jit(solution)/shard_map/joined_projection/pallas_call | solution.py:312
  57.1 2.1 %hand_over.1 = (bf16[4,2304]{1,0:T(4,128)(2,1)}, bf16[32,256]{1,0:T(8,128)(2,1)}, bf16[2304,256]{1,0:T(8,128)(2,1)}) custom-call(bf16[4,2304]{1,0:T(4,128)(2,1)} %get-tuple-element.6.refs_0_, bf16[32,256]{1,0:T(8,128)(2,1)} %get-tuple-element.7.refs_1_, bf16[2304,256]{1,0:T(8,128)(2,1)} %get-tuple-element.8.refs_2_), custom_call_target="tpu_custom_call" | custom-call | tf_op jit(solution)/shard_map/hand_over/pallas_call | solution.py:358

commit v6 on v5

--- a/solution.py
+++ b/solution.py
@@ -235,7 +235,7 @@
     )
     for k in range(Y * Z):
         start = k // Y % 4 * 64 + k % Y * 16 + k // 16 * TOK
-        grad[k // 8, k % 8 * TOK : k % 8 * TOK + TOK, :] = product[start : start + TOK, :]
+        grad[k // 8, k % 8 * TOK : k % 8 * TOK + TOK, :] = product[start : start + TOK, :].astype(BF16)
     by_row = [
         send(
             grad.at[lax.rem(row + d, ROWS)], grad_in.at[d - 1],
@@ -259,10 +259,10 @@
     ]
     stores[0].start()
 
-    total = grad[row]
+    total = grad[row].astype(F32)
     for i, copy in enumerate(by_row):
         copy.wait_recv()
-        total += grad_in[i]
+        total += grad_in[i].astype(F32)
     input_ref[...] = total.astype(BF16)
     stores[1].start()
 
@@ -342,8 +342,8 @@
             pltpu.VMEM((3, CLASS, TOK, columns), BF16),
             pltpu.VMEM((CLASS, TOK, columns), BF16),
             pltpu.VMEM((Z - 1, TOK, columns), BF16),
-            pltpu.VMEM((ROWS, inputs.shape[0] // ROWS, depth), F32),
-            pltpu.VMEM((ROWS - 1, inputs.shape[0] // ROWS, depth), F32),
+            pltpu.VMEM((ROWS, inputs.shape[0] // ROWS, depth), BF16),
+            pltpu.VMEM((ROWS - 1, inputs.shape[0] // ROWS, depth), BF16),
             dma((len(WINDOW),)), dma((len(WINDOW),)), dma((len(FAR),)), dma((len(FAR),)),
             dma((len(FAR),)), dma((len(FAR),)), dma((6,)), dma((6,)), dma((21,)), dma((21,)),
             dma((pieces, Y - 1)), dma((pieces, Y - 1)), dma((pieces, 4)), dma((pieces, 4)),

time: 59.3 us -> 59.3 us (level); the launches traced: 59.2 us -> 58.5 us
  Pallas kernels: 58.5 us -> 57.8 us
    pallas_call x1, Pallas kernels: 56.4 us -> 55.7 us  [local(): pl.pallas_call(kernel, out_shape=(jax.ShapeDtypeStruct(out_grad.shape, BF...]
where the time goes in v6:
time: 59.3 us; the launch traced here: 58.5 us
  Pallas kernels  57.8 us (97%)
  between operations  0.64 us (1%)
    pallas_call x1, Pallas kernels, local(): pl.pallas_call(kernel, out_shape=(jax.ShapeDtypeStruct(out_grad.shape, BF...  55.7 us
    pallas_call x1, Pallas kernels, local(): pl.pallas_call(hand_over, out_shape=tuple((jax.ShapeDtypeStruct(a.shape,...  2.11 us

profile of v6, /device:TPU:1, one launch (start us, length us, event | category | flops | bytes accessed | tf_op | source)
XLA Modules:
  0.0 58.5 jit_solution(14293107545032715546)
XLA Ops:
  0.6 55.7 %joined_projection.1 = (bf16[4,2304]{1,0:T(4,128)(2,1)}, bf16[32,256]{1,0:T(8,128)(2,1)}, bf16[2304,256]{1,0:T(8,128)(2,1)}) custom-call(bf16[256,256]{1,0:T(8,128)(2,1)} %x_hbm.1, bf16[2304,256]{1,0:T(8,128)(2,1)} %w_hbm.1, bf16[4,2304]{1,0:T(4,128)(2,1)} %g_hbm.1), custom_call_target="tpu_custom_call" | custom-call | tf_op jit(solution)/shard_map/joined_projection/pallas_call | solution.py:312
  56.4 2.1 %hand_over.1 = (bf16[4,2304]{1,0:T(4,128)(2,1)}, bf16[32,256]{1,0:T(8,128)(2,1)}, bf16[2304,256]{1,0:T(8,128)(2,1)}) custom-call(bf16[4,2304]{1,0:T(4,128)(2,1)} %get-tuple-element.6.refs_0_, bf16[32,256]{1,0:T(8,128)(2,1)} %get-tuple-element.7.refs_1_, bf16[2304,256]{1,0:T(8,128)(2,1)} %get-tuple-element.8.refs_2_), custom_call_target="tpu_custom_call" | custom-call | tf_op jit(solution)/shard_map/hand_over/pallas_call | solution.py:358
